TPU v7x, 32 devices: a whole 2x2x4 slice. The times are simulated.
32 devices in a mesh: outer: 8 (over z, x), inner: 4 (over y, core).
Axes of the slice: x: 2, y: 2, z: 4, core: 2. Of those that a mesh axis runs over, the one named last changes fastest.
Arguments:
- queries: bfloat16 [32768, 1024], P(('outer', 'inner')), may hold values from -6 to 6
- keys: bfloat16 [32768, 1024], P(('outer', 'inner')), may hold values from -6 to 6
- values: bfloat16 [32768, 1024], P(('outer', 'inner')), may hold values from -6 to 6
- norm_gain: float32 [1024], replicated, may hold values from 0.1 to 1.9
- out_weight: bfloat16 [1024, 2048], replicated, may hold values from -0.1875 to 0.1875
Outputs:
- mixed: bfloat16 [32768, 2048], P(('outer', 'inner'))
All inputs are finite; a program needn't handle non-finite values.
Results may differ from a plain program's by a relative error of at most 0.0058.
Values sent between devices are 32-bit elements; how exact they have to be, the bound alone decides.
A program may use at most 320 MiB of HBM per device.

v0:
```python
import functools

import jax
import jax.numpy as jnp
from jax import lax
from jax.experimental import pallas as pl
from jax.experimental.pallas import tpu as pltpu
from jax.sharding import PartitionSpec as P

H = 8
DH = 128
PAIRS = H // 2
PW = 2 * DH
CHUNK = 256
ROWS = 512
TILE = 512
F32 = jnp.float32
BF16 = jnp.bfloat16
MESH = pl.DeviceIdType.MESH
ORDER = (1, 3, 2, 0)
PART = DH // 2
PARTS = (slice(0, PART), slice(PART, DH))


def scan_kernel(
    n_outer, n_inner, q_hbm, k_hbm, v_hbm, w_hbm, gain_hbm, normed, w,
    gain, q, k, v, pre, low, diag, local, pair_buf, chip, up_buf, zs, zb, zx, down_src, down_buf, fwd, pd,
    load_sem, w_sem, gain_sem, pair_send, pair_recv, up_send, up_recv, z_send, z_recv,
    down_send, down_recv, fwd_send, fwd_recv,
):
    tok = q.shape[0]
    blocks = tok // CHUNK
    groups = n_outer * n_inner // H
    rounds = (groups - 1).bit_length()
    me = lax.axis_index("outer") * n_inner + lax.axis_index("inner")
    group, place = me // H, me % H
    c, e = place // 2, place % 2

    def device(index):
        return (index // n_inner, index % n_inner)

    def remote(src, dst, send, recv, target):
        return pltpu.make_async_remote_copy(
            src_ref=src, dst_ref=dst, send_sem=send, recv_sem=recv,
            device_id=device(target), device_id_type=MESH,
        )

    partner = group * H + 2 * c + (1 - e)

    def mate(j):
        return group * H + 2 * j + e

    def cols(j, width):
        return pl.ds(pl.multiple_of(j * width, width), width)

    def load(which, hbm, vmem, j):
        return pltpu.make_async_copy(hbm.at[:, cols(j, PW)], vmem.at[:, cols(j, PW)], load_sem.at[which, j])

    barrier = pltpu.get_barrier_semaphore()

    def greet(target):
        pl.semaphore_signal(barrier, inc=1, device_id=device(target), device_id_type=MESH)

    greet(partner)
    for s in range(1, PAIRS):
        greet(mate((c + s) % PAIRS))
    expected = PAIRS
    for d in range(rounds):
        step = 1 << d
        up, down = group + step < groups, group >= step

        @pl.when(up)
        def _():
            greet(me + step * H)

        @pl.when(down)
        def _():
            greet(me - step * H)

        expected = expected + jnp.where(up, 1, 0) + jnp.where(down, 1, 0)

    for s in range(PAIRS):
        j = (c + ORDER[s]) % PAIRS
        load(0, k_hbm, k, j).start()
        load(1, v_hbm, v, j).start()
    for j in range(PAIRS):
        load(2, q_hbm, q, j).start()
    whole_w = pltpu.make_async_copy(w_hbm, w, w_sem)
    whole_w.start()
    whole_gain = pltpu.make_async_copy(gain_hbm, gain, gain_sem)
    whole_gain.start()
    diag[...] = jnp.zeros_like(diag)

    def pair_copy(j):
        return remote(local.at[2 * j + 1 - e], pair_buf.at[j], pair_send.at[j], pair_recv.at[j], partner)

    def part(p):
        return pl.ds(p * PART, PART)

    def up_copy(j, slot, p):
        return remote(
            chip.at[j, part(p)], up_buf.at[slot, part(p)], up_send.at[p, j], up_recv.at[p, slot], mate(j)
        )

    def chip_sum(s):
        j = (c + ORDER[s]) % PAIRS
        pair_copy(j).wait_recv()
        total = local[2 * j + e] + pair_buf[j]
        if ORDER[s]:
            chip[j] = total
            for p in range(2):
                up_copy(j, c, p).start()
        else:
            up_buf[c] = total

    for s in range(PAIRS):
        j = (c + ORDER[s]) % PAIRS
        load(0, k_hbm, k, j).wait()
        load(1, v_hbm, v, j).wait()
        sums = [None, None]
        for b in range(blocks):
            at = (pl.ds(b * CHUNK, CHUNK), cols(j, PW))
            both = lax.dot_general(k[at], v[at], (((0,), (0,)), ((), ())), preferred_element_type=F32)
            for half in range(2):
                own = both[half * DH:(half + 1) * DH, half * DH:(half + 1) * DH]
                sums[half] = own if b == 0 else sums[half] + own
                if b + 1 < blocks:
                    low[2 * j + half, b] = sums[half].astype(BF16)
        local[2 * j] = sums[0]
        local[2 * j + 1] = sums[1]
        if s == 0:
            pl.semaphore_wait(barrier, expected)
        pair_copy(j).start()
        if s > 0:
            chip_sum(s - 1)
    chip_sum(PAIRS - 1)

    for j in range(PAIRS):
        load(2, q_hbm, q, j).wait()

    causal = lax.broadcasted_iota(jnp.int32, (CHUNK, CHUNK), 0) >= lax.broadcasted_iota(
        jnp.int32, (CHUNK, CHUNK), 1
    )

    def causal_part(h, _):
        weights = []
        for b in range(blocks):
            at = (pl.ds(b * CHUNK, CHUNK), cols(h, DH))
            scores = lax.dot_general(q[at], k[at], (((1,), (1,)), ((), ())), preferred_element_type=F32)
            weights.append(jnp.where(causal, scores, 0.0).astype(BF16))
        for b in range(blocks):
            at = (pl.ds(b * CHUNK, CHUNK), cols(h, DH))
            inside = jnp.dot(weights[b], v[at], preferred_element_type=F32)
            if b > 0:
                inside = inside + jnp.dot(q[at], low[h, b - 1], preferred_element_type=F32)
            pre[at] = inside
        return 0

    done = 0

    def work(heads):
        nonlocal done
        until = min(H, done + heads)
        if until > done:
            lax.fori_loop(done, until, causal_part, 0)
        done = until

    def z_copy(d, target, p):
        return remote(zs.at[d, part(p)], zb.at[d, part(p)], z_send.at[p, d], z_recv.at[p, d], target)

    def z_start(d, p):
        @pl.when(group + (1 << d) < groups)
        def _():
            z_copy(d, me + (1 << d) * H, p).start()

    def z_take(d, p):
        rows = PARTS[p]

        @pl.when(group >= 1 << d)
        def _():
            z_copy(d, me - (1 << d) * H, p).wait_recv()
            zx[rows] = zx[rows] + zb[d, rows]

        if d + 1 < rounds:
            @pl.when(group >= 1 << d)
            def _():
                zs[d + 1, rows] = zs[d, rows] + zb[d, rows]

            @pl.when(group < 1 << d)
            def _():
                zs[d + 1, rows] = zs[d, rows]

    def down_copy(j, slot, p):
        return remote(
            down_src.at[j, part(p)], down_buf.at[slot, part(p)], down_send.at[p, j], down_recv.at[p, slot], mate(j)
        )

    def down_start(p):
        rows = PARTS[p]
        running = zx[rows]
        for i in range(PAIRS):
            down_src[i, rows] = running
            if i + 1 < PAIRS:
                running = running + up_buf[i, rows]
        for s in range(1, PAIRS):
            down_copy((c + s) % PAIRS, c, p).start()
        down_buf[c, rows] = down_src[c, rows]

    work(2)
    zx[...] = jnp.zeros_like(zx)
    for p in range(2):
        rows = PARTS[p]
        for s in range(1, PAIRS):
            j = (c + s) % PAIRS
            up_copy(j, j, p).wait_recv()
        zs[0, rows] = up_buf[0, rows] + up_buf[1, rows] + up_buf[2, rows] + up_buf[3, rows]
        z_start(0, p)
        work(1)
    for d in range(rounds):
        for p in range(2):
            z_take(d, p)
            if d + 1 < rounds:
                z_start(d + 1, p)
            else:
                down_start(p)
            work(1)
    work(H)

    def fwd_copy(j, p):
        return remote(fwd.at[j, part(p)], pd.at[j, part(p)], fwd_send.at[p, j], fwd_recv.at[p, j], partner)

    def spread(s, p):
        j = (c + s) % PAIRS
        rows = PARTS[p]
        if s:
            down_copy(j, j, p).wait_recv()
        first = down_buf[j, rows]
        fwd[j, rows] = jnp.where(e == 0, first + local[2 * j, rows], first)
        fwd_copy(j, p).start()
        at = pl.ds(pl.multiple_of(e * DH + p * PART, PART), PART)
        half = pl.ds(pl.multiple_of(e * DH, DH), DH)
        diag[s, at, half] = jnp.where(e == 1, first + pair_buf[j, rows], first).astype(BF16)

    def norm(s):
        j = (c + s) % PAIRS
        for p in range(2):
            fwd_copy(j, p).wait_recv()
        half = pl.ds(pl.multiple_of((1 - e) * DH, DH), DH)
        diag[s, half, half] = pd[j].astype(BF16)
        carried = diag[s]
        for b in range(blocks):
            rows = pl.ds(b * CHUNK, CHUNK)
            both = pre[rows, cols(j, PW)] + jnp.dot(q[rows, cols(j, PW)], carried, preferred_element_type=F32)
            for i in range(2):
                attended = both[:, i * DH:(i + 1) * DH]
                mean_square = jnp.mean(attended * attended, axis=-1, keepdims=True)
                scaled = attended * lax.rsqrt(mean_square + 1e-06) * gain[:, cols(2 * j + i, DH)]
                normed[rows, cols(2 * j + i, DH)] = scaled.astype(BF16)

    whole_gain.wait()
    for s in range(PAIRS):
        spread(s, 0)
    spread(0, 1)
    for s in range(1, PAIRS):
        spread(s, 1)
        norm(s - 1)
    norm(PAIRS - 1)
    whole_w.wait()

    for s in range(PAIRS):
        j = (c + s) % PAIRS
        pair_copy(j).wait_send()
        for p in range(2):
            fwd_copy(j, p).wait_send()
            if s:
                up_copy(j, c, p).wait_send()
                down_copy(j, c, p).wait_send()
    for d in range(rounds):
        @pl.when(group + (1 << d) < groups)
        def _():
            for p in range(2):
                z_copy(d, me + (1 << d) * H, p).wait_send()


def scan_and_norm(n_outer, n_inner, queries, keys, values, norm_gain, out_weight):
    tok, width = queries.shape
    rounds = max(1, (n_outer * n_inner // H - 1).bit_length())
    state = lambda count: pltpu.VMEM((count, DH, DH), F32)
    sems = lambda *shape: pltpu.SemaphoreType.DMA(shape)
    whole = pltpu.VMEM((tok, width), BF16)
    vmem = pl.BlockSpec(memory_space=pltpu.VMEM)
    held = [pltpu.with_memory_space_constraint(x, pltpu.HBM) for x in (queries, keys, values, out_weight, norm_gain.reshape(1, width))]
    return pl.pallas_call(
        functools.partial(scan_kernel, n_outer, n_inner),
        out_shape=(
            jax.ShapeDtypeStruct((tok, width), BF16),
            jax.ShapeDtypeStruct(out_weight.shape, BF16),
        ),
        in_specs=[pl.BlockSpec(memory_space=pl.ANY)] * 5,
        out_specs=(vmem, vmem),
        scratch_shapes=[
            pltpu.VMEM((1, width), F32), whole, whole, whole, pltpu.VMEM((tok, width), F32),
            pltpu.VMEM((H, max(1, tok // CHUNK - 1), DH, DH), BF16), pltpu.VMEM((PAIRS, PW, PW), BF16),
            state(H), state(PAIRS), state(PAIRS), state(PAIRS),
            state(rounds), state(rounds), pltpu.VMEM((DH, DH), F32),
            state(PAIRS), state(PAIRS), state(PAIRS), state(PAIRS),
            sems(3, PAIRS), pltpu.SemaphoreType.DMA, pltpu.SemaphoreType.DMA, sems(PAIRS), sems(PAIRS), sems(2, PAIRS), sems(2, PAIRS),
            sems(2, rounds), sems(2, rounds), sems(2, PAIRS), sems(2, PAIRS), sems(2, PAIRS), sems(2, PAIRS),
        ],
        compiler_params=pltpu.CompilerParams(
            collective_id=0, has_side_effects=True, vmem_limit_bytes=32 * 1024 * 1024
        ),
        name="scan_and_norm",
    )(*held)


def project_kernel(normed, w, out_hbm, out, out_sem):
    tok, model = out.shape
    copies = []
    for r in range(tok // ROWS):
        for n in range(model // TILE):
            rows, at = pl.ds(r * ROWS, ROWS), pl.ds(n * TILE, TILE)
            out[rows, at] = jnp.dot(normed[rows, :], w[:, at], preferred_element_type=F32).astype(BF16)
            copy = pltpu.make_async_copy(out.at[rows, at], out_hbm.at[rows, at], out_sem.at[r, n])
            copy.start()
            copies.append(copy)
    for copy in copies:
        copy.wait()


def project(normed, out_weight):
    tok, model = normed.shape[0], out_weight.shape[1]
    return pl.pallas_call(
        project_kernel,
        out_shape=jax.ShapeDtypeStruct((tok, model), BF16),
        in_specs=[pl.BlockSpec(memory_space=pltpu.VMEM)] * 2,
        out_specs=pl.BlockSpec(memory_space=pl.ANY),
        scratch_shapes=[
            pltpu.VMEM((tok, model), BF16),
            pltpu.SemaphoreType.DMA((tok // ROWS, model // TILE)),
        ],
        compiler_params=pltpu.CompilerParams(vmem_limit_bytes=20 * 1024 * 1024),
        name="project",
    )(normed, out_weight)


def solution(mesh):
    n_outer, n_inner = mesh.shape["outer"], mesh.shape["inner"]

    def on_device(queries, keys, values, norm_gain, out_weight):
        normed, weight = scan_and_norm(n_outer, n_inner, queries, keys, values, norm_gain, out_weight)
        return project(normed, weight)

    rows = P(("outer", "inner"), None)
    return jax.shard_map(
        on_device,
        mesh=mesh,
        in_specs=(rows, rows, rows, P(), P()),
        out_specs=rows,
        check_vma=False,
    )
```

profile of v0, /device:TPU:17, one launch (start us, length us, event | category | flops | bytes accessed | tf_op | source)
XLA Modules:
  0.0 27.6 jit_solution(9136526606004734555)
XLA Ops:
  0.0 22.2 %scan_and_norm.1 = (bf16[1024,1024]{1,0:T(8,128)(2,1)S(1)}, bf16[1024,2048]{1,0:T(8,128)(2,1)S(1)}) custom-call(bf16[1024,1024]{1,0:T(8,128)(2,1)} %q_hbm.1, bf16[1024,1024]{1,0:T(8,128)(2,1)} %k_hbm.1, bf16[1024,1024]{1,0:T(8,128)(2,1)} %v_hbm.1, bf16[1024,2048]{1,0:T(8,128)(2,1)} %w_hbm.1, f32[1,1024]{1,0:T(1,128)} %bitcast.1), custom_call_target="tpu_custom_call" | custom-call | tf_op jit(solution)/shard_map/scan_and_norm/pallas_call | solution.py:293
  22.2 5.4 %project.1 = bf16[1024,2048]{1,0:T(8,128)(2,1)} custom-call(bf16[1024,1024]{1,0:T(8,128)(2,1)S(1)} %get-tuple-element.7.normed, bf16[1024,2048]{1,0:T(8,128)(2,1)S(1)} %get-tuple-element.8.w), custom_call_target="tpu_custom_call" | custom-call | tf_op jit(solution)/shard_map/project/pallas_call | solution.py:333
where the time goes:
time: 27.8 us; the launch traced here: 27.6 us
  Pallas kernels  27.6 us (99%)
    pallas_call x1, Pallas kernels, scan_and_norm(): pl.pallas_call(functools.partial(scan_kernel, n_outer, n_inner), out_shap...  22.2 us
    pallas_call x1, Pallas kernels, project(): pl.pallas_call(project_kernel, out_shape=jax.ShapeDtypeStruct((tok, model...  5.37 us

commit v1 on v0

--- a/solution.py
+++ b/solution.py
@@ -11,8 +11,9 @@
 DH = 128
 PAIRS = H // 2
 PW = 2 * DH
+C = 128
 CHUNK = 256
-ROWS = 512
+ROWS = 256
 TILE = 512
 F32 = jnp.float32
 BF16 = jnp.bfloat16
@@ -24,12 +25,12 @@
 
 def scan_kernel(
     n_outer, n_inner, q_hbm, k_hbm, v_hbm, w_hbm, gain_hbm, normed, w,
-    gain, q, k, v, pre, low, diag, local, pair_buf, chip, up_buf, zs, zb, zx, down_src, down_buf, fwd, pd,
+    gain, q, k, v, pre, low, diag, averaging, local, pair_buf, chip, up_buf, zs, zb, zx, down_src, down_buf, fwd, pd,
     load_sem, w_sem, gain_sem, pair_send, pair_recv, up_send, up_recv, z_send, z_recv,
     down_send, down_recv, fwd_send, fwd_recv,
 ):
     tok = q.shape[0]
-    blocks = tok // CHUNK
+    blocks = tok // C
     groups = n_outer * n_inner // H
     rounds = (groups - 1).bit_length()
     me = lax.axis_index("outer") * n_inner + lax.axis_index("inner")
@@ -90,6 +91,9 @@
     whole_gain = pltpu.make_async_copy(gain_hbm, gain, gain_sem)
     whole_gain.start()
     diag[...] = jnp.zeros_like(diag)
+    averaging[...] = jnp.zeros_like(averaging)
+    for i in range(2):
+        averaging[i * DH:(i + 1) * DH, i * DH:(i + 1) * DH] = jnp.full((DH, DH), 1.0 / DH, BF16)
 
     def pair_copy(j):
         return remote(local.at[2 * j + 1 - e], pair_buf.at[j], pair_send.at[j], pair_recv.at[j], partner)
@@ -119,10 +123,9 @@
         load(1, v_hbm, v, j).wait()
         sums = [None, None]
         for b in range(blocks):
-            at = (pl.ds(b * CHUNK, CHUNK), cols(j, PW))
-            both = lax.dot_general(k[at], v[at], (((0,), (0,)), ((), ())), preferred_element_type=F32)
             for half in range(2):
-                own = both[half * DH:(half + 1) * DH, half * DH:(half + 1) * DH]
+                at = (pl.ds(b * C, C), cols(2 * j + half, DH))
+                own = lax.dot_general(k[at], v[at], (((0,), (0,)), ((), ())), preferred_element_type=F32)
                 sums[half] = own if b == 0 else sums[half] + own
                 if b + 1 < blocks:
                     low[2 * j + half, b] = sums[half].astype(BF16)
@@ -138,22 +141,21 @@
     for j in range(PAIRS):
         load(2, q_hbm, q, j).wait()
 
-    causal = lax.broadcasted_iota(jnp.int32, (CHUNK, CHUNK), 0) >= lax.broadcasted_iota(
-        jnp.int32, (CHUNK, CHUNK), 1
+    causal = lax.broadcasted_iota(jnp.int32, (C, C), 0) >= lax.broadcasted_iota(
+        jnp.int32, (C, C), 1
     )
 
     def causal_part(h, _):
-        weights = []
+        left = []
         for b in range(blocks):
-            at = (pl.ds(b * CHUNK, CHUNK), cols(h, DH))
+            at = (pl.ds(b * C, C), cols(h, DH))
             scores = lax.dot_general(q[at], k[at], (((1,), (1,)), ((), ())), preferred_element_type=F32)
-            weights.append(jnp.where(causal, scores, 0.0).astype(BF16))
+            weights = jnp.where(causal, scores, 0.0).astype(BF16)
+            left.append(jnp.concatenate([weights, q[at]], axis=1) if b else weights)
         for b in range(blocks):
-            at = (pl.ds(b * CHUNK, CHUNK), cols(h, DH))
-            inside = jnp.dot(weights[b], v[at], preferred_element_type=F32)
-            if b > 0:
-                inside = inside + jnp.dot(q[at], low[h, b - 1], preferred_element_type=F32)
-            pre[at] = inside
+            at = (pl.ds(b * C, C), cols(h, DH))
+            right = jnp.concatenate([v[at], low[h, b - 1]], axis=0) if b else v[at]
+            pre[at] = jnp.dot(left[b], right, preferred_element_type=F32)
         return 0
 
     done = 0
@@ -248,14 +250,12 @@
         half = pl.ds(pl.multiple_of((1 - e) * DH, DH), DH)
         diag[s, half, half] = pd[j].astype(BF16)
         carried = diag[s]
-        for b in range(blocks):
-            rows = pl.ds(b * CHUNK, CHUNK)
-            both = pre[rows, cols(j, PW)] + jnp.dot(q[rows, cols(j, PW)], carried, preferred_element_type=F32)
-            for i in range(2):
-                attended = both[:, i * DH:(i + 1) * DH]
-                mean_square = jnp.mean(attended * attended, axis=-1, keepdims=True)
-                scaled = attended * lax.rsqrt(mean_square + 1e-06) * gain[:, cols(2 * j + i, DH)]
-                normed[rows, cols(2 * j + i, DH)] = scaled.astype(BF16)
+        for b in range(tok // CHUNK):
+            at = (pl.ds(b * CHUNK, CHUNK), cols(j, PW))
+            attended = pre[at] + jnp.dot(q[at], carried, preferred_element_type=F32)
+            mean_square = jnp.dot((attended * attended).astype(BF16), averaging[...], preferred_element_type=F32)
+            scaled = attended * lax.rsqrt(mean_square + 1e-06) * gain[:, cols(j, PW)]
+            normed[at] = scaled.astype(BF16)
 
     whole_gain.wait()
     for s in range(PAIRS):
@@ -300,8 +300,8 @@
         out_specs=(vmem, vmem),
         scratch_shapes=[
             pltpu.VMEM((1, width), F32), whole, whole, whole, pltpu.VMEM((tok, width), F32),
-            pltpu.VMEM((H, max(1, tok // CHUNK - 1), DH, DH), BF16), pltpu.VMEM((PAIRS, PW, PW), BF16),
-            state(H), state(PAIRS), state(PAIRS), state(PAIRS),
+            pltpu.VMEM((H, max(1, tok // C - 1), DH, DH), BF16), pltpu.VMEM((PAIRS, PW, PW), BF16),
+            pltpu.VMEM((PW, PW), BF16), state(H), state(PAIRS), state(PAIRS), state(PAIRS),
             state(rounds), state(rounds), pltpu.VMEM((DH, DH), F32),
             state(PAIRS), state(PAIRS), state(PAIRS), state(PAIRS),
             sems(3, PAIRS), pltpu.SemaphoreType.DMA, pltpu.SemaphoreType.DMA, sems(PAIRS), sems(PAIRS), sems(2, PAIRS), sems(2, PAIRS),

time: 27.8 us -> 27.6 us (level)
  Pallas kernels: 27.6 us -> 27.2 us
    pallas_call x1, Pallas kernels: 22.2 us -> 21.8 us  [scan_and_norm(): pl.pallas_call(functools.partial(scan_kernel, n_outer, n_inner), out_shap...]
where the time goes in v1:
time: 27.6 us; the launch traced here: 27.2 us
  Pallas kernels  27.2 us (99%)
    pallas_call x1, Pallas kernels, scan_and_norm(): pl.pallas_call(functools.partial(scan_kernel, n_outer, n_inner), out_shap...  21.8 us
    pallas_call x1, Pallas kernels, project(): pl.pallas_call(project_kernel, out_shape=jax.ShapeDtypeStruct((tok, model...  5.35 us

profile of v1, /device:TPU:17, one launch (start us, length us, event | category | flops | bytes accessed | tf_op | source)
XLA Modules:
  0.0 27.2 jit_solution(13349208720458279988)
XLA Ops:
  0.0 21.8 %scan_and_norm.1 = (bf16[1024,1024]{1,0:T(8,128)(2,1)S(1)}, bf16[1024,2048]{1,0:T(8,128)(2,1)S(1)}) custom-call(bf16[1024,1024]{1,0:T(8,128)(2,1)} %q_hbm.1, bf16[1024,1024]{1,0:T(8,128)(2,1)} %k_hbm.1, bf16[1024,1024]{1,0:T(8,128)(2,1)} %v_hbm.1, bf16[1024,2048]{1,0:T(8,128)(2,1)} %w_hbm.1, f32[1,1024]{1,0:T(1,128)} %bitcast.1), custom_call_target="tpu_custom_call" | custom-call | tf_op jit(solution)/shard_map/scan_and_norm/pallas_call | solution.py:293
  21.8 5.4 %project.1 = bf16[1024,2048]{1,0:T(8,128)(2,1)} custom-call(bf16[1024,1024]{1,0:T(8,128)(2,1)S(1)} %get-tuple-element.7.normed, bf16[1024,2048]{1,0:T(8,128)(2,1)S(1)} %get-tuple-element.8.w), custom_call_target="tpu_custom_call" | custom-call | tf_op jit(solution)/shard_map/project/pallas_call | solution.py:333

commit v2 on v1

--- a/solution.py
+++ b/solution.py
@@ -84,12 +84,6 @@
         j = (c + ORDER[s]) % PAIRS
         load(0, k_hbm, k, j).start()
         load(1, v_hbm, v, j).start()
-    for j in range(PAIRS):
-        load(2, q_hbm, q, j).start()
-    whole_w = pltpu.make_async_copy(w_hbm, w, w_sem)
-    whole_w.start()
-    whole_gain = pltpu.make_async_copy(gain_hbm, gain, gain_sem)
-    whole_gain.start()
     diag[...] = jnp.zeros_like(diag)
     averaging[...] = jnp.zeros_like(averaging)
     for i in range(2):
@@ -136,8 +130,13 @@
         pair_copy(j).start()
         if s > 0:
             chip_sum(s - 1)
+    for j in range(PAIRS):
+        load(2, q_hbm, q, j).start()
     chip_sum(PAIRS - 1)
-
+    whole_w = pltpu.make_async_copy(w_hbm, w, w_sem)
+    whole_w.start()
+    whole_gain = pltpu.make_async_copy(gain_hbm, gain, gain_sem)
+    whole_gain.start()
     for j in range(PAIRS):
         load(2, q_hbm, q, j).wait()
 

time: 27.6 us -> 27.6 us (level)
  no operation moved by 1% of the time
where the time goes in v2:
time: 27.6 us; the launch traced here: 27.2 us
  Pallas kernels  27.2 us (99%)
    pallas_call x1, Pallas kernels, scan_and_norm(): pl.pallas_call(functools.partial(scan_kernel, n_outer, n_inner), out_shap...  21.8 us
    pallas_call x1, Pallas kernels, project(): pl.pallas_call(project_kernel, out_shape=jax.ShapeDtypeStruct((tok, model...  5.35 us

profile of v2, /device:TPU:17, one launch (start us, length us, event | category | flops | bytes accessed | tf_op | source)
XLA Modules:
  0.0 27.2 jit_solution(17754653585893071782)
XLA Ops:
  0.0 21.8 %scan_and_norm.1 = (bf16[1024,1024]{1,0:T(8,128)(2,1)S(1)}, bf16[1024,2048]{1,0:T(8,128)(2,1)S(1)}) custom-call(bf16[1024,1024]{1,0:T(8,128)(2,1)} %q_hbm.1, bf16[1024,1024]{1,0:T(8,128)(2,1)} %k_hbm.1, bf16[1024,1024]{1,0:T(8,128)(2,1)} %v_hbm.1, bf16[1024,2048]{1,0:T(8,128)(2,1)} %w_hbm.1, f32[1,1024]{1,0:T(1,128)} %bitcast.1), custom_call_target="tpu_custom_call" | custom-call | tf_op jit(solution)/shard_map/scan_and_norm/pallas_call | solution.py:292
  21.8 5.4 %project.1 = bf16[1024,2048]{1,0:T(8,128)(2,1)} custom-call(bf16[1024,1024]{1,0:T(8,128)(2,1)S(1)} %get-tuple-element.7.normed, bf16[1024,2048]{1,0:T(8,128)(2,1)S(1)} %get-tuple-element.8.w), custom_call_target="tpu_custom_call" | custom-call | tf_op jit(solution)/shard_map/project/pallas_call | solution.py:332

commit v3 on v2

--- a/solution.py
+++ b/solution.py
@@ -18,7 +18,6 @@
 F32 = jnp.float32
 BF16 = jnp.bfloat16
 MESH = pl.DeviceIdType.MESH
-ORDER = (1, 3, 2, 0)
 PART = DH // 2
 PARTS = (slice(0, PART), slice(PART, DH))
 
@@ -81,7 +80,7 @@
         expected = expected + jnp.where(up, 1, 0) + jnp.where(down, 1, 0)
 
     for s in range(PAIRS):
-        j = (c + ORDER[s]) % PAIRS
+        j = (c + s + 1) % PAIRS
         load(0, k_hbm, k, j).start()
         load(1, v_hbm, v, j).start()
     diag[...] = jnp.zeros_like(diag)
@@ -100,39 +99,46 @@
             chip.at[j, part(p)], up_buf.at[slot, part(p)], up_send.at[p, j], up_recv.at[p, slot], mate(j)
         )
 
-    def chip_sum(s):
-        j = (c + ORDER[s]) % PAIRS
-        pair_copy(j).wait_recv()
-        total = local[2 * j + e] + pair_buf[j]
-        if ORDER[s]:
-            chip[j] = total
-            for p in range(2):
-                up_copy(j, c, p).start()
-        else:
-            up_buf[c] = total
-
-    for s in range(PAIRS):
-        j = (c + ORDER[s]) % PAIRS
-        load(0, k_hbm, k, j).wait()
-        load(1, v_hbm, v, j).wait()
-        sums = [None, None]
-        for b in range(blocks):
-            for half in range(2):
-                at = (pl.ds(b * C, C), cols(2 * j + half, DH))
-                own = lax.dot_general(k[at], v[at], (((0,), (0,)), ((), ())), preferred_element_type=F32)
-                sums[half] = own if b == 0 else sums[half] + own
-                if b + 1 < blocks:
-                    low[2 * j + half, b] = sums[half].astype(BF16)
-        local[2 * j] = sums[0]
-        local[2 * j + 1] = sums[1]
-        if s == 0:
-            pl.semaphore_wait(barrier, expected)
-        pair_copy(j).start()
-        if s > 0:
-            chip_sum(s - 1)
+    def first_pass(s, _):
+        @pl.when(s < PAIRS)
+        def _():
+            j = (c + s + 1) % PAIRS
+            load(0, k_hbm, k, j).wait()
+            load(1, v_hbm, v, j).wait()
+            sums = [None, None]
+            for b in range(blocks):
+                for half in range(2):
+                    at = (pl.ds(b * C, C), cols(2 * j + half, DH))
+                    own = lax.dot_general(k[at], v[at], (((0,), (0,)), ((), ())), preferred_element_type=F32)
+                    sums[half] = own if b == 0 else sums[half] + own
+                    if b + 1 < blocks:
+                        low[2 * j + half, b] = sums[half].astype(BF16)
+            local[2 * j] = sums[0]
+            local[2 * j + 1] = sums[1]
+            pair_copy(j).start()
+
+        @pl.when(s > 0)
+        def _():
+            j = (c + s) % PAIRS
+            pair_copy(j).wait_recv()
+            total = local[2 * j + e] + pair_buf[j]
+
+            @pl.when(s < PAIRS)
+            def _():
+                chip[j] = total
+                for p in range(2):
+                    up_copy(j, c, p).start()
+
+            @pl.when(s == PAIRS)
+            def _():
+                up_buf[c] = total
+
+        return 0
+
     for j in range(PAIRS):
         load(2, q_hbm, q, j).start()
-    chip_sum(PAIRS - 1)
+    pl.semaphore_wait(barrier, expected)
+    lax.fori_loop(0, PAIRS + 1, first_pass, 0)
     whole_w = pltpu.make_async_copy(w_hbm, w, w_sem)
     whole_w.start()
     whole_gain = pltpu.make_async_copy(gain_hbm, gain, gain_sem)
@@ -144,7 +150,7 @@
         jnp.int32, (C, C), 1
     )
 
-    def causal_part(h, _):
+    def causal_part(h):
         left = []
         for b in range(blocks):
             at = (pl.ds(b * C, C), cols(h, DH))
@@ -155,16 +161,6 @@
             at = (pl.ds(b * C, C), cols(h, DH))
             right = jnp.concatenate([v[at], low[h, b - 1]], axis=0) if b else v[at]
             pre[at] = jnp.dot(left[b], right, preferred_element_type=F32)
-        return 0
-
-    done = 0
-
-    def work(heads):
-        nonlocal done
-        until = min(H, done + heads)
-        if until > done:
-            lax.fori_loop(done, until, causal_part, 0)
-        done = until
 
     def z_copy(d, target, p):
         return remote(zs.at[d, part(p)], zb.at[d, part(p)], z_send.at[p, d], z_recv.at[p, d], target)
@@ -207,25 +203,36 @@
             down_copy((c + s) % PAIRS, c, p).start()
         down_buf[c, rows] = down_src[c, rows]
 
-    work(2)
-    zx[...] = jnp.zeros_like(zx)
-    for p in range(2):
+    def up_take(p):
         rows = PARTS[p]
         for s in range(1, PAIRS):
             j = (c + s) % PAIRS
             up_copy(j, j, p).wait_recv()
         zs[0, rows] = up_buf[0, rows] + up_buf[1, rows] + up_buf[2, rows] + up_buf[3, rows]
-        z_start(0, p)
-        work(1)
-    for d in range(rounds):
+
+    def exchange(i):
         for p in range(2):
-            z_take(d, p)
-            if d + 1 < rounds:
-                z_start(d + 1, p)
+            if i == 0:
+                up_take(p)
+            else:
+                z_take(i - 1, p)
+            if i < rounds:
+                z_start(i, p)
             else:
                 down_start(p)
-            work(1)
-    work(H)
+
+    zx[...] = jnp.zeros_like(zx)
+    stride = 2 if rounds < 4 else 1
+
+    def tick(h, _):
+        causal_part(h)
+        for i in range(rounds + 1):
+            @pl.when(h == min(H - 1, 1 + i * stride))
+            def _():
+                exchange(i)
+        return 0
+
+    lax.fori_loop(0, H, tick, 0)
 
     def fwd_copy(j, p):
         return remote(fwd.at[j, part(p)], pd.at[j, part(p)], fwd_send.at[p, j], fwd_recv.at[p, j], partner)
@@ -233,8 +240,11 @@
     def spread(s, p):
         j = (c + s) % PAIRS
         rows = PARTS[p]
-        if s:
+
+        @pl.when(s > 0)
+        def _():
             down_copy(j, j, p).wait_recv()
+
         first = down_buf[j, rows]
         fwd[j, rows] = jnp.where(e == 0, first + local[2 * j, rows], first)
         fwd_copy(j, p).start()
@@ -257,13 +267,23 @@
             normed[at] = scaled.astype(BF16)
 
     whole_gain.wait()
-    for s in range(PAIRS):
+    def take_first(s, _):
         spread(s, 0)
-    spread(0, 1)
-    for s in range(1, PAIRS):
-        spread(s, 1)
-        norm(s - 1)
-    norm(PAIRS - 1)
+        return 0
+
+    def take_second(s, _):
+        @pl.when(s < PAIRS)
+        def _():
+            spread(s, 1)
+
+        @pl.when(s > 0)
+        def _():
+            norm(s - 1)
+
+        return 0
+
+    lax.fori_loop(0, PAIRS, take_first, 0)
+    lax.fori_loop(0, PAIRS + 1, take_second, 0)
     whole_w.wait()
 
     for s in range(PAIRS):
@@ -315,16 +335,23 @@
 
 def project_kernel(normed, w, out_hbm, out, out_sem):
     tok, model = out.shape
-    copies = []
-    for r in range(tok // ROWS):
+    chunks = tok // ROWS
+
+    def store(r):
+        rows = pl.ds(pl.multiple_of(r * ROWS, ROWS), ROWS)
+        return pltpu.make_async_copy(out.at[rows, :], out_hbm.at[rows, :], out_sem.at[r])
+
+    def chunk(r, _):
+        rows = pl.ds(pl.multiple_of(r * ROWS, ROWS), ROWS)
         for n in range(model // TILE):
-            rows, at = pl.ds(r * ROWS, ROWS), pl.ds(n * TILE, TILE)
+            at = pl.ds(n * TILE, TILE)
             out[rows, at] = jnp.dot(normed[rows, :], w[:, at], preferred_element_type=F32).astype(BF16)
-            copy = pltpu.make_async_copy(out.at[rows, at], out_hbm.at[rows, at], out_sem.at[r, n])
-            copy.start()
-            copies.append(copy)
-    for copy in copies:
-        copy.wait()
+        store(r).start()
+        return 0
+
+    lax.fori_loop(0, chunks, chunk, 0)
+    for r in range(chunks):
+        store(r).wait()
 
 
 def project(normed, out_weight):
@@ -336,7 +363,7 @@
         out_specs=pl.BlockSpec(memory_space=pl.ANY),
         scratch_shapes=[
             pltpu.VMEM((tok, model), BF16),
-            pltpu.SemaphoreType.DMA((tok // ROWS, model // TILE)),
+            pltpu.SemaphoreType.DMA((tok // ROWS,)),
         ],
         compiler_params=pltpu.CompilerParams(vmem_limit_bytes=20 * 1024 * 1024),
         name="project",

time: 27.6 us -> 29.4 us (1.065)
  Pallas kernels: 27.2 us -> 29.1 us
    pallas_call x1, Pallas kernels: 21.8 us -> 23.1 us  [scan_and_norm(): pl.pallas_call(functools.partial(scan_kernel, n_outer, n_inner), out_shap...]
    pallas_call x1, Pallas kernels: 5.35 us -> 6.01 us  [project(): pl.pallas_call(project_kernel, out_shape=jax.ShapeDtypeStruct((tok, model...]
where the time goes in v3:
time: 29.4 us; the launch traced here: 29.1 us
  Pallas kernels  29.1 us (99%)
    pallas_call x1, Pallas kernels, scan_and_norm(): pl.pallas_call(functools.partial(scan_kernel, n_outer, n_inner), out_shap...  23.1 us
    pallas_call x1, Pallas kernels, project(): pl.pallas_call(project_kernel, out_shape=jax.ShapeDtypeStruct((tok, model...  6.01 us

profile of v3, /device:TPU:17, one launch (start us, length us, event | category | flops | bytes accessed | tf_op | source)
XLA Modules:
  0.0 29.1 jit_solution(9633050224615860396)
XLA Ops:
  0.0 23.1 %scan_and_norm.1 = (bf16[1024,1024]{1,0:T(8,128)(2,1)S(1)}, bf16[1024,2048]{1,0:T(8,128)(2,1)S(1)}) custom-call(bf16[1024,1024]{1,0:T(8,128)(2,1)} %q_hbm.1, bf16[1024,1024]{1,0:T(8,128)(2,1)} %k_hbm.1, bf16[1024,1024]{1,0:T(8,128)(2,1)} %v_hbm.1, bf16[1024,2048]{1,0:T(8,128)(2,1)} %w_hbm.1, f32[1,1024]{1,0:T(1,128)} %bitcast.1), custom_call_target="tpu_custom_call" | custom-call | tf_op jit(solution)/shard_map/scan_and_norm/pallas_call | solution.py:312
  23.1 6.0 %project.1 = bf16[1024,2048]{1,0:T(8,128)(2,1)} custom-call(bf16[1024,1024]{1,0:T(8,128)(2,1)S(1)} %get-tuple-element.7.normed, bf16[1024,2048]{1,0:T(8,128)(2,1)S(1)} %get-tuple-element.8.w), custom_call_target="tpu_custom_call" | custom-call | tf_op jit(solution)/shard_map/project/pallas_call | solution.py:359

commit v4 on v2

--- a/solution.py
+++ b/solution.py
@@ -25,7 +25,7 @@
 
 def scan_kernel(
     n_outer, n_inner, q_hbm, k_hbm, v_hbm, w_hbm, gain_hbm, normed, w,
-    gain, q, k, v, pre, low, diag, averaging, local, pair_buf, chip, up_buf, zs, zb, zx, down_src, down_buf, fwd, pd,
+    gain, q, k, v, pre, diag, averaging, local, pair_buf, chip, up_buf, zs, zb, zx, down_src, down_buf, fwd, pd,
     load_sem, w_sem, gain_sem, pair_send, pair_recv, up_send, up_recv, z_send, z_recv,
     down_send, down_recv, fwd_send, fwd_recv,
 ):
@@ -115,16 +115,11 @@
         j = (c + ORDER[s]) % PAIRS
         load(0, k_hbm, k, j).wait()
         load(1, v_hbm, v, j).wait()
-        sums = [None, None]
-        for b in range(blocks):
-            for half in range(2):
-                at = (pl.ds(b * C, C), cols(2 * j + half, DH))
-                own = lax.dot_general(k[at], v[at], (((0,), (0,)), ((), ())), preferred_element_type=F32)
-                sums[half] = own if b == 0 else sums[half] + own
-                if b + 1 < blocks:
-                    low[2 * j + half, b] = sums[half].astype(BF16)
-        local[2 * j] = sums[0]
-        local[2 * j + 1] = sums[1]
+        both = lax.dot_general(
+            k[:, cols(j, PW)], v[:, cols(j, PW)], (((0,), (0,)), ((), ())), preferred_element_type=F32
+        )
+        local[2 * j] = both[:DH, :DH]
+        local[2 * j + 1] = both[DH:, DH:]
         if s == 0:
             pl.semaphore_wait(barrier, expected)
         pair_copy(j).start()
@@ -151,9 +146,14 @@
             scores = lax.dot_general(q[at], k[at], (((1,), (1,)), ((), ())), preferred_element_type=F32)
             weights = jnp.where(causal, scores, 0.0).astype(BF16)
             left.append(jnp.concatenate([weights, q[at]], axis=1) if b else weights)
+        states = []
+        for b in range(blocks - 1):
+            at = (pl.ds(b * C, C), cols(h, DH))
+            own = lax.dot_general(k[at], v[at], (((0,), (0,)), ((), ())), preferred_element_type=F32)
+            states.append(states[-1] + own if b else own)
         for b in range(blocks):
             at = (pl.ds(b * C, C), cols(h, DH))
-            right = jnp.concatenate([v[at], low[h, b - 1]], axis=0) if b else v[at]
+            right = jnp.concatenate([v[at], states[b - 1].astype(BF16)], axis=0) if b else v[at]
             pre[at] = jnp.dot(left[b], right, preferred_element_type=F32)
         return 0
 
@@ -216,7 +216,7 @@
             up_copy(j, j, p).wait_recv()
         zs[0, rows] = up_buf[0, rows] + up_buf[1, rows] + up_buf[2, rows] + up_buf[3, rows]
         z_start(0, p)
-        work(1)
+    work(2)
     for d in range(rounds):
         for p in range(2):
             z_take(d, p)
@@ -224,7 +224,8 @@
                 z_start(d + 1, p)
             else:
                 down_start(p)
-            work(1)
+        if d + 1 < rounds:
+            work(3)
     work(H)
 
     def fwd_copy(j, p):
@@ -299,7 +300,7 @@
         out_specs=(vmem, vmem),
         scratch_shapes=[
             pltpu.VMEM((1, width), F32), whole, whole, whole, pltpu.VMEM((tok, width), F32),
-            pltpu.VMEM((H, max(1, tok // C - 1), DH, DH), BF16), pltpu.VMEM((PAIRS, PW, PW), BF16),
+            pltpu.VMEM((PAIRS, PW, PW), BF16),
             pltpu.VMEM((PW, PW), BF16), state(H), state(PAIRS), state(PAIRS), state(PAIRS),
             state(rounds), state(rounds), pltpu.VMEM((DH, DH), F32),
             state(PAIRS), state(PAIRS), state(PAIRS), state(PAIRS),

time: 27.6 us -> 28.6 us (1.036)
  Pallas kernels: 27.2 us -> 28.4 us
    pallas_call x1, Pallas kernels: 21.8 us -> 23.1 us  [scan_and_norm(): pl.pallas_call(functools.partial(scan_kernel, n_outer, n_inner), out_shap...]
where the time goes in v4:
time: 28.6 us; the launch traced here: 28.4 us
  Pallas kernels  28.4 us (99%)
    pallas_call x1, Pallas kernels, scan_and_norm(): pl.pallas_call(functools.partial(scan_kernel, n_outer, n_inner), out_shap...  23.1 us
    pallas_call x1, Pallas kernels, project(): pl.pallas_call(project_kernel, out_shape=jax.ShapeDtypeStruct((tok, model...  5.35 us

profile of v4, /device:TPU:17, one launch (start us, length us, event | category | flops | bytes accessed | tf_op | source)
XLA Modules:
  0.0 28.4 jit_solution(3506033062194722128)
XLA Ops:
  0.0 23.1 %scan_and_norm.1 = (bf16[1024,1024]{1,0:T(8,128)(2,1)S(1)}, bf16[1024,2048]{1,0:T(8,128)(2,1)S(1)}) custom-call(bf16[1024,1024]{1,0:T(8,128)(2,1)} %q_hbm.1, bf16[1024,1024]{1,0:T(8,128)(2,1)} %k_hbm.1, bf16[1024,1024]{1,0:T(8,128)(2,1)} %v_hbm.1, bf16[1024,2048]{1,0:T(8,128)(2,1)} %w_hbm.1, f32[1,1024]{1,0:T(1,128)} %bitcast.1), custom_call_target="tpu_custom_call" | custom-call | tf_op jit(solution)/shard_map/scan_and_norm/pallas_call | solution.py:293
  23.1 5.4 %project.1 = bf16[1024,2048]{1,0:T(8,128)(2,1)} custom-call(bf16[1024,1024]{1,0:T(8,128)(2,1)S(1)} %get-tuple-element.7.normed, bf16[1024,2048]{1,0:T(8,128)(2,1)S(1)} %get-tuple-element.8.w), custom_call_target="tpu_custom_call" | custom-call | tf_op jit(solution)/shard_map/project/pallas_call | solution.py:333

commit v5 on v2

--- a/solution.py
+++ b/solution.py
@@ -216,7 +216,7 @@
             up_copy(j, j, p).wait_recv()
         zs[0, rows] = up_buf[0, rows] + up_buf[1, rows] + up_buf[2, rows] + up_buf[3, rows]
         z_start(0, p)
-        work(1)
+    work(2)
     for d in range(rounds):
         for p in range(2):
             z_take(d, p)
@@ -224,7 +224,8 @@
                 z_start(d + 1, p)
             else:
                 down_start(p)
-            work(1)
+        if d + 1 < rounds:
+            work(3)
     work(H)
 
     def fwd_copy(j, p):

time: 27.6 us -> 28.7 us (1.040)
  Pallas kernels: 27.2 us -> 28.5 us
    pallas_call x1, Pallas kernels: 21.8 us -> 23.2 us  [scan_and_norm(): pl.pallas_call(functools.partial(scan_kernel, n_outer, n_inner), out_shap...]
where the time goes in v5:
time: 28.7 us; the launch traced here: 28.5 us
  Pallas kernels  28.5 us (99%)
    pallas_call x1, Pallas kernels, scan_and_norm(): pl.pallas_call(functools.partial(scan_kernel, n_outer, n_inner), out_shap...  23.2 us
    pallas_call x1, Pallas kernels, project(): pl.pallas_call(project_kernel, out_shape=jax.ShapeDtypeStruct((tok, model...  5.35 us

profile of v5, /device:TPU:17, one launch (start us, length us, event | category | flops | bytes accessed | tf_op | source)
XLA Modules:
  0.0 28.5 jit_solution(17569421238357906647)
XLA Ops:
  0.0 23.2 %scan_and_norm.1 = (bf16[1024,1024]{1,0:T(8,128)(2,1)S(1)}, bf16[1024,2048]{1,0:T(8,128)(2,1)S(1)}) custom-call(bf16[1024,1024]{1,0:T(8,128)(2,1)} %q_hbm.1, bf16[1024,1024]{1,0:T(8,128)(2,1)} %k_hbm.1, bf16[1024,1024]{1,0:T(8,128)(2,1)} %v_hbm.1, bf16[1024,2048]{1,0:T(8,128)(2,1)} %w_hbm.1, f32[1,1024]{1,0:T(1,128)} %bitcast.1), custom_call_target="tpu_custom_call" | custom-call | tf_op jit(solution)/shard_map/scan_and_norm/pallas_call | solution.py:293
  23.2 5.4 %project.1 = bf16[1024,2048]{1,0:T(8,128)(2,1)} custom-call(bf16[1024,1024]{1,0:T(8,128)(2,1)S(1)} %get-tuple-element.7.normed, bf16[1024,2048]{1,0:T(8,128)(2,1)S(1)} %get-tuple-element.8.w), custom_call_target="tpu_custom_call" | custom-call | tf_op jit(solution)/shard_map/project/pallas_call | solution.py:333
